TPU v7x, 32 devices: a whole 2x2x4 slice. The times are simulated.
32 devices in a mesh: groups: 2 (over x), ep: 16 (over z, y, core).
Axes of the slice: x: 2, y: 2, z: 4, core: 2. Of those that a mesh axis runs over, the one named last changes fastest.
Arguments:
- tokens: bfloat16 [2048, 2048], P(('groups', 'ep')), parts along dimension 0, may hold values from -6 to 6
- routes: int32 [2048, 8], P(('groups', 'ep')), parts along dimension 0, may hold values from 0 to 15, all different within a row; in each aligned block of 64 rows (0 to 63, 64 to 127, ...) at most 32 rows name the same one
- gate_codes: int32 [2048, 8], P(('groups', 'ep')), parts along dimension 0, may hold values from 1 to 65535
- trainer_experts: int32 [16], replicated, may hold values from 0 to 15, each once
- placement: int32 [4, 5], replicated, may hold values from 0 to 15, as said below
- w_gate: bfloat16 [16, 2048, 768], P('ep'), may hold values from -0.125 to 0.125
- w_up: bfloat16 [16, 2048, 768], P('ep'), may hold values from -0.125 to 0.125
- w_down: bfloat16 [16, 2048, 768], P('ep'), may hold values from -0.21875 to 0.21875
Outputs:
- mixed: bfloat16 [2048, 2048], P(('groups', 'ep')), parts along dimension 0
- rollout_gate: bfloat16 [32, 5, 2048, 192], P(('groups', 'ep')), parts along dimension 0
- rollout_up: bfloat16 [32, 5, 2048, 192], P(('groups', 'ep')), parts along dimension 0
- rollout_down: bfloat16 [32, 5, 2048, 192], P(('groups', 'ep')), parts along dimension 0
There are 2 independent parts, one for each index of `groups`. A program takes and returns all parts, laid end to end along the dimension named above; an argument that names none is the same for every part. Nothing has to cross between parts.
Inputs may be any that keep to these rules, and one draw needn't show every extreme that they name: `routes`: in the rows of one device no expert is named by more than 32 rows, and each row names 8 different experts. `trainer_experts`: each expert is held by exactly one trainer slot. `placement`: every expert appears in some slot; 4 slots, one in each rollout group at a drawn position, repeat an expert that also appears elsewhere, possibly in the same group.
All inputs are finite; a program needn't handle non-finite values.
Results may differ from a plain program's by a relative error of at most 0.005.
Values may be sent and summed in bfloat16 or wider, within the bound.
A program may use at most 256 MiB of HBM per device.

v0:
```python
import jax
import jax.numpy as jnp
from jax import lax
from jax.sharding import PartitionSpec as P


def compact_rows(flags, capacity):
    return jnp.nonzero(flags, size=capacity, fill_value=0)[0].astype(jnp.int32)


def expert_outputs(picked, weights):
    slot_gate, slot_up, slot_down = weights
    gate_proj = jnp.einsum("srd,sdf->srf", picked, slot_gate, preferred_element_type=jnp.float32)
    up_proj = jnp.einsum("srd,sdf->srf", picked, slot_up, preferred_element_type=jnp.float32)
    hidden = (jax.nn.silu(gate_proj) * up_proj).astype(jnp.bfloat16)
    return jnp.einsum("srf,sdf->srd", hidden, slot_down, preferred_element_type=jnp.float32)


def contribute(all_tokens, all_routes, gate_values, weights, slot_experts, live, capacity):
    hits = (all_routes[None, :, :] == slot_experts[:, None, None]) & live[:, None, None]
    row_weight = jnp.sum(jnp.where(hits, gate_values[None, :, :], 0.0), axis=2)
    chosen = jnp.any(hits, axis=2)
    rows_index = jax.vmap(lambda flags: compact_rows(flags, capacity))(chosen)
    counts = jnp.sum(chosen.astype(jnp.int32), axis=1)
    valid = jnp.arange(capacity, dtype=jnp.int32)[None, :] < counts[:, None]
    row_gates = jnp.where(valid, jnp.take_along_axis(row_weight, rows_index, axis=1), 0.0)
    picked = all_tokens[rows_index]
    outputs = expert_outputs(picked, weights) * row_gates[:, :, None]
    width = all_tokens.shape[1]
    totals = jnp.zeros((all_tokens.shape[0], width), jnp.float32)
    return totals.at[rows_index.reshape(-1)].add(outputs.reshape(-1, width))


def body(tokens, routes, gate_codes, trainer_experts, placement, w_gate, w_up, w_down):
    device_count = lax.axis_size("ep")
    position = lax.axis_index("ep")
    quarters = 4
    slot_count = placement.shape[1]
    expert_count = trainer_experts.shape[0]
    hidden_width = w_gate.shape[2]
    quarter_width = hidden_width // quarters
    local_rows = tokens.shape[0]
    home_cap = local_rows // 2
    capacity = device_count * home_cap
    all_tokens, all_routes, all_codes = (
        lax.all_gather(tokens, "ep", axis=0, tiled=True),
        lax.all_gather(routes, "ep", axis=0, tiled=True),
        lax.all_gather(gate_codes, "ep", axis=0, tiled=True),
    )
    codes = all_codes.astype(jnp.float32)
    gate_values = codes / jnp.sum(codes, axis=1, keepdims=True)
    owner_slot = (
        jnp.zeros((expert_count,), jnp.int32)
        .at[trainer_experts]
        .set(jnp.arange(expert_count, dtype=jnp.int32))
    )
    moved_gate, moved_up, moved_down = (
        lax.all_to_all(w_gate, "ep", split_axis=1, concat_axis=0, tiled=True),
        lax.all_to_all(w_up, "ep", split_axis=1, concat_axis=0, tiled=True),
        lax.all_to_all(w_down, "ep", split_axis=1, concat_axis=0, tiled=True),
    )
    dest_source = jnp.repeat(owner_slot[placement], quarters, axis=0)
    quarter_of = (jnp.arange(device_count, dtype=jnp.int32) % quarters)[:, None]

    def pick(matrix):
        blocks = matrix.reshape(expert_count, matrix.shape[1], quarters, quarter_width)
        return blocks[dest_source, :, quarter_of, :]

    rollout_gate, rollout_up, rollout_down = (
        lax.all_to_all(pick(moved_gate), "ep", split_axis=0, concat_axis=2, tiled=True),
        lax.all_to_all(pick(moved_up), "ep", split_axis=0, concat_axis=2, tiled=True),
        lax.all_to_all(pick(moved_down), "ep", split_axis=0, concat_axis=2, tiled=True),
    )
    mixed = None
    quad = position // quarters
    slot_experts = placement[quad]
    flat_slots = placement.reshape(-1)
    slots_total = flat_slots.shape[0]
    matches = flat_slots[None, :] == jnp.arange(expert_count, dtype=jnp.int32)[:, None]
    first_slot = jnp.min(
        jnp.where(matches, jnp.arange(slots_total, dtype=jnp.int32)[None, :], slots_total), axis=1
    )
    live = first_slot[slot_experts] == quad * slot_count + jnp.arange(slot_count, dtype=jnp.int32)
    weights = (rollout_gate[0], rollout_up[0], rollout_down[0])
    totals = contribute(all_tokens, all_routes, gate_values, weights, slot_experts, live, capacity)
    mixed = lax.psum_scatter(totals, "ep", scatter_dimension=0, tiled=True).astype(jnp.bfloat16)
    return (mixed, rollout_gate, rollout_up, rollout_down)


def solution(mesh):
    placed = (
        P(("groups", "ep"), None),
        P(("groups", "ep"), None),
        P(("groups", "ep"), None),
        P(),
        P(),
        P("ep", None, None),
        P("ep", None, None),
        P("ep", None, None),
    )
    return jax.shard_map(
        body,
        mesh=mesh,
        in_specs=placed,
        out_specs=(
            P(("groups", "ep"), None),
            P(("groups", "ep"), None, None, None),
            P(("groups", "ep"), None, None, None),
            P(("groups", "ep"), None, None, None),
        ),
        check_vma=False,
    )
```

profile of v0, /device:TPU:8, one launch (start us, length us, event | category | flops | bytes accessed | tf_op | source)
XLA Modules:
  0.0 903.5 jit_solution(13117900863164892376)
XLA Ops:
  7.2 6.9 copy.121
  14.6 31.6 %reduce.17 = bf16[2048,768]{1,0:T(8,128)(2,1)S(1)} reduce(bf16[2048,1,768]{2,1,0:T(2,128)(2,1)} %bitcast.112, bf16[]{:T(256)} %broadcast.540), dimensions={1}, to_apply=%bitcast.107.reduce_sub_computation | reduce | bytes 6291458
  49.7 6.3 all-to-all-start
  56.0 6.9 copy.120
  62.9 33.3 %reduce.18 = bf16[2048,768]{1,0:T(8,128)(2,1)} reduce(bf16[2048,1,768]{2,1,0:T(2,128)(2,1)} %bitcast.114, bf16[]{:T(256)} %broadcast.540), dimensions={1}, to_apply=%bitcast.106.reduce_sub_computation | reduce | bytes 6291458
  96.2 6.4 reshape.529
  102.6 21.8 %all-to-all-done = bf16[16,2,49152]{2,1,0:T(2,128)(2,1)S(1)} async-done(((bf16[16,2,49152]{2,1,0:T(2,128)(2,1)}), bf16[16,2,49152]{2,1,0:T(2,128)(2,1)S(1)}, u32[]{:S(2)}, u32[]{:S(2)}) %all-to-all-start) | async-done | bytes 3145760 | tf_op jit(solution)/shard_map/all_to_all | solution.py:58
  126.0 6.7 all-to-all-start.2
  132.8 6.9 copy.119
  139.7 33.3 %reduce.16 = bf16[2048,768]{1,0:T(8,128)(2,1)} reduce(bf16[2048,1,768]{2,1,0:T(2,128)(2,1)} %bitcast.113, bf16[]{:T(256)} %broadcast.540), dimensions={1}, to_apply=%bitcast.105.reduce_sub_computation | reduce | bytes 6291458
  172.9 6.3 reshape.531
  179.3 21.7 %all-to-all-done.2 = bf16[16,2,49152]{2,1,0:T(2,128)(2,1)S(1)} async-done(((bf16[16,2,49152]{2,1,0:T(2,128)(2,1)}), bf16[16,2,49152]{2,1,0:T(2,128)(2,1)S(1)}, u32[]{:S(2)}, u32[]{:S(2)}) %all-to-all-start.2) | async-done | bytes 3145760 | tf_op jit(solution)/shard_map/all_to_all | solution.py:59
  201.0 6.4 all-to-all-start.4
  209.4 11.5 %reshape.528 = bf16[2048,1,768]{2,1,0:T(2,128)(2,1)} reshape(bf16[16,2,49152]{2,1,0:T(2,128)(2,1)} %copy-done.2) | data formatting | bytes 6291456
  220.9 34.1 %bitcast_reduce_fusion.2 = bf16[2048,768]{1,0:T(8,128)(2,1)S(1)} fusion(bf16[2048,1,768]{2,1,0:T(2,128)(2,1)} %reshape.528), kind=kLoop, calls=%fused_computation.84 | loop fusion | bytes 6291456 | tf_op jit(solution)/shard_map/all_to_all | solution.py:58
  255.0 4.8 reshape.513
  259.8 5.9 copy.82
  269.1 6.7 all-to-all-done.4
  275.8 7.2 all-to-all-start.1
  283.0 7.6 reshape.530
  290.6 34.1 %bitcast_reduce_fusion.1 = bf16[2048,768]{1,0:T(8,128)(2,1)S(1)} fusion(bf16[2048,1,768]{2,1,0:T(2,128)(2,1)} %reshape.530), kind=kLoop, calls=%fused_computation.83 | loop fusion | bytes 6291456 | tf_op jit(solution)/shard_map/all_to_all | solution.py:59
  324.7 4.8 reshape.514
  329.5 5.9 copy.86
  338.8 29.2 %all-to-all-done.1 = bf16[16,5,128,192]{2,3,1,0:T(8,128)(2,1)} async-done(((bf16[16,5,128,192]{2,3,1,0:T(8,128)(2,1)}), bf16[16,5,128,192]{2,3,1,0:T(8,128)(2,1)}, u32[]{:S(2)}, u32[]{:S(2)}) %all-to-all-start.1) | async-done | bytes 3932192 | tf_op jit(solution)/shard_map/all_to_all | solution.py:70
  368.0 6.6 all-to-all-start.3
  375.3 11.5 %reshape.532 = bf16[2048,1,768]{2,1,0:T(2,128)(2,1)} reshape(bf16[16,2,49152]{2,1,0:T(2,128)(2,1)} %all-to-all-done.4) | data formatting | bytes 6291456
  386.8 34.1 %bitcast_reduce_fusion = bf16[2048,768]{1,0:T(8,128)(2,1)S(1)} fusion(bf16[2048,1,768]{2,1,0:T(2,128)(2,1)} %reshape.532), kind=kLoop, calls=%fused_computation.82 | loop fusion | bytes 6291456 | tf_op jit(solution)/shard_map/all_to_all | solution.py:60
  420.9 4.8 reshape.515
  425.6 5.9 copy.90
  435.0 50.0 %all-to-all-done.3 = bf16[16,5,128,192]{2,3,1,0:T(8,128)(2,1)} async-done(((bf16[16,5,128,192]{2,3,1,0:T(8,128)(2,1)}), bf16[16,5,128,192]{2,3,1,0:T(8,128)(2,1)}, u32[]{:S(2)}, u32[]{:S(2)}) %all-to-all-start.3) | async-done | bytes 3932192 | tf_op jit(solution)/shard_map/all_to_all | solution.py:71
  485.1 6.7 all-to-all-start.5
  491.9 97.0 %all-gather = s32[16,64,8]{1,2,0:T(8,128)S(1)} all-gather(s32[1,64,8]{1,2,0:T(8,128)S(1)} %bitcast.123), channel_id=1, replica_groups=mesh['groups'=2,'ep'=16] {'ep'}, dimensions={0}, use_global_device_ids=true | all-gather | bytes 34816 | tf_op jit(solution)/shard_map/all_gather | solution.py:47
  592.2 35.8 %scatter_custom_fusion.2 = s32[2560]{0:T(1024)S(1)} fusion(s32[5120]{0:T(1024)S(1)} %reshape.497, s32[5120]{0:T(1024)S(1)} %broadcast.481, s32[]{:T(128)} %constant.106.clone.1), kind=kCustom, calls=%fused_computation.60 | custom fusion | flops 5120 | bytes 10244
  630.2 16.9 %all-gather.1 = s32[16,64,8]{1,2,0:T(8,128)S(1)} all-gather(s32[1,64,8]{1,2,0:T(8,128)S(1)} %bitcast.124), channel_id=1, replica_groups=mesh['groups'=2,'ep'=16] {'ep'}, dimensions={0}, use_global_device_ids=true | all-gather | bytes 34816 | tf_op jit(solution)/shard_map/all_gather | solution.py:48
  647.4 16.3 %gather_fusion.6 = f32[2560]{0:T(1024)S(1)} fusion(f32[5,1024]{1,0:T(8,128)S(1)} %select_reduce_fusion, s32[2560]{0:T(1024)S(1)} %reshape.475), kind=kCustom, calls=%fused_computation.6 | custom fusion | bytes 40960 | tf_op jit(solution)/shard_map/jit(take_along_axis)/gather | solution.py:26
  664.1 22.9 %gather_fusion.1 = bf16[2560,2048]{1,0:T(8,128)(2,1)} fusion(bf16[1024,2048]{1,0:T(8,128)(2,1)} %all-gather.4.cloned.1.call-done, s32[3072]{0:T(1024)S(1)} %pad_clamp_fusion), kind=kCustom, calls=%fused_computation.1 | custom fusion | bytes 20981760 | tf_op jit(solution)/shard_map/gather | solution.py:27
  687.0 6.6 copy.83
  693.5 7.0 squeeze.13
  700.6 6.6 copy.87
  707.1 7.1 squeeze.14
  714.2 6.6 copy.91
  720.8 7.2 squeeze.15
  728.0 8.7 fusion.22
  736.7 15.6 %broadcast_multiply_fusion = f32[5,512,2048]{2,1,0:T(8,128)} fusion(f32[5,512]{1,0:T(8,128)S(1)} %select_select_fusion, bf16[5,2048,192]{1,2,0:T(8,128)(2,1)} %squeeze.15, f32[5,512,192]{1,2,0:T(8,128)S(1)} %fusion.22, bf16[5,512,2048]{2,1,0:T(8,128)(2,1)} %bitcast.110, bf16[5,2048,192]{1,2,0:T(8,128)(2,1)} %squeeze.14), kind=kOutput, calls=%fused_computation.10 | convolution fusion | flops 4034723840 | bytes 41297920 | tf_op jit(solution)/shard_map/srf,sdf->srd/dot_general | solution.py:16
  752.3 37.4 %scatter_custom_fusion.1 = f32[1024,2048]{1,0:T(8,128)} fusion(s32[2560]{0:T(1024)S(1)} %fusion.9, f32[2560,2048]{1,0:T(8,128)} %bitcast.111, f32[]{:T(128)} %constant.103.clone.1), kind=kCustom, calls=%fused_computation.11 | custom fusion | flops 5242880 | bytes 8389120 | tf_op jit(solution)/shard_map/scatter-add | solution.py:31
  794.3 5.0 copy_bitcast_fusion.1
  799.3 5.0 copy_bitcast_fusion.2
  804.3 90.4 %reduce-scatter.2.cloned.1.call-done = f32[64,2048]{1,0:T(8,128)} async-done(((f32[1024,2048]{1,0:T(8,128)}), f32[64,2048]{1,0:T(8,128)}) %reduce-scatter.2.cloned.1.call-update) | async-done | bytes 524304 | tf_op jit(solution)/shard_map/reduce_scatter | solution.py:86
  (97 shorter events, 31.4 us)
Async XLA Ops:
  49.7 74.6 %all-to-all-start = ((bf16[16,2,49152]{2,1,0:T(2,128)(2,1)}), bf16[16,2,49152]{2,1,0:T(2,128)(2,1)S(1)}, u32[]{:S(2)}, u32[]{:S(2)}) async-start(bf16[16,2,49152]{2,1,0:T(2,128)(2,1)} %reshape.527), calls=%async_computation | async-start | bytes 6291456 | tf_op jit(solution)/shard_map/all_to_all | solution.py:58
  124.4 1.7 copy-start.2
  126.0 75.0 %all-to-all-start.2 = ((bf16[16,2,49152]{2,1,0:T(2,128)(2,1)}), bf16[16,2,49152]{2,1,0:T(2,128)(2,1)S(1)}, u32[]{:S(2)}, u32[]{:S(2)}) async-start(bf16[16,2,49152]{2,1,0:T(2,128)(2,1)} %reshape.529), calls=%async_computation.2 | async-start | bytes 6291456 | tf_op jit(solution)/shard_map/all_to_all | solution.py:59
  179.3 28.2 %copy-start.3 = (s32[4,5]{1,0:T(4,128)S(1)}, s32[4,5]{1,0:T(4,128)}, u32[]{:S(2)}) copy-start(s32[4,5]{1,0:T(4,128)} %param.12) | copy-start | bytes 244
  179.3 28.3 %copy-start.8 = (s32[16]{0:T(128)S(1)}, s32[16]{0:T(128)}, u32[]{:S(2)}) copy-start(s32[16]{0:T(128)} %param.11) | copy-start | bytes 196
  201.0 6.6 copy-start
  201.0 74.8 %all-to-all-start.4 = ((bf16[16,2,49152]{2,1,0:T(2,128)(2,1)}), bf16[16,2,49152]{2,1,0:T(2,128)(2,1)}, u32[]{:S(2)}, u32[]{:S(2)}) async-start(bf16[16,2,49152]{2,1,0:T(2,128)(2,1)} %reshape.531), calls=%async_computation.4 | async-start | bytes 6291456 | tf_op jit(solution)/shard_map/all_to_all | solution.py:60
  275.8 7.2 copy-start.1
  275.8 92.2 %all-to-all-start.1 = ((bf16[16,5,128,192]{2,3,1,0:T(8,128)(2,1)}), bf16[16,5,128,192]{2,3,1,0:T(8,128)(2,1)}, u32[]{:S(2)}, u32[]{:S(2)}) async-start(bf16[16,5,128,192]{2,3,1,0:T(8,128)(2,1)} %bitcast.117), calls=%async_computation.1 | async-start | bytes 7864320 | tf_op jit(solution)/shard_map/all_to_all | solution.py:70
  368.0 117.0 %all-to-all-start.3 = ((bf16[16,5,128,192]{2,3,1,0:T(8,128)(2,1)}), bf16[16,5,128,192]{2,3,1,0:T(8,128)(2,1)}, u32[]{:S(2)}, u32[]{:S(2)}) async-start(bf16[16,5,128,192]{2,3,1,0:T(8,128)(2,1)} %bitcast.116), calls=%async_computation.3 | async-start | bytes 7864320 | tf_op jit(solution)/shard_map/all_to_all | solution.py:71
  374.6 289.5 %all-gather.4.cloned.1.call-start = ((), (), s32[]{:S(2)}) async-start(), calls=%async_computation.7 | async-start | bytes 4456448 | tf_op jit(solution)/shard_map/all_gather | solution.py:46
  485.1 6.8 copy-start.4
  485.1 106.9 %copy-start.7 = (s32[2]{0:T(128)S(1)}, s32[2]{0:T(128)}, u32[]{:S(2)}) copy-start(s32[2]{0:T(128)} %constant.124) | copy-start | bytes 28
  485.1 107.0 %copy-start.6 = (s32[2]{0:T(128)S(1)}, s32[2]{0:T(128)}, u32[]{:S(2)}) copy-start(s32[2]{0:T(128)} %constant.127) | copy-start | bytes 28
  485.1 145.1 %copy-start.5 = (s32[64,8]{0,1:T(8,128)S(1)}, s32[64,8]{0,1:T(8,128)}, u32[]{:S(2)}) copy-start(s32[64,8]{0,1:T(8,128)} %param.10) | copy-start | bytes 6148
  485.1 229.2 %all-to-all-start.5 = ((bf16[16,5,128,192]{2,3,1,0:T(8,128)(2,1)}), bf16[16,5,128,192]{2,3,1,0:T(8,128)(2,1)}, u32[]{:S(2)}, u32[]{:S(2)}) async-start(bf16[16,5,128,192]{2,3,1,0:T(8,128)(2,1)} %bitcast.115), calls=%async_computation.5 | async-start | bytes 7864320 | tf_op jit(solution)/shard_map/all_to_all | solution.py:72
  491.8 402.9 %reduce-scatter.2.cloned.1.call-start = ((), (), s32[]{:S(2)}) async-start(), calls=%async_computation.8 | async-start | bytes 8912896 | tf_op jit(solution)/shard_map/reduce_scatter | solution.py:86
Sparse Core Ops, SparseCore 0:
  377.6 95.5 all-gather.3
  789.8 104.8 reduce-scatter.1
where the time goes:
time: 914 us; the launch traced here: 904 us
  local copies, waits for them, and re-layouts  313 us (34%)
  waiting for transfers between devices  220 us (24%)
  other arithmetic  178 us (19%)
  blocking collectives  114 us (12%)
  starting transfers between devices  40.4 us (4%)
  matrix products  24.2 us (3%)
  between operations  14.7 us (2%)
    unnamed x10, other arithmetic  134 us
    all_gather x1, blocking collectives, body(): lax.all_gather(routes, 'ep', axis=0, tiled=True)  97 us
    reduce_scatter x1, waiting for transfers between devices, body(): lax.psum_scatter(totals, 'ep', scatter_dimension=0, tiled=True)  90.4 us
    unnamed x33, local copies, waits for them, and re-layouts  69.9 us
    all_to_all x1, waiting for transfers between devices, body(): lax.all_to_all(pick(moved_up), 'ep', split_axis=0, concat_axis=2, tiled=T...  50 us
    scatter-add x1, other arithmetic, contribute(): return totals.at[rows_index.reshape(-1)].add(outputs.reshape(-1, width))  37.4 us
    all_to_all x1, local copies, waits for them, and re-layouts, body(): lax.all_to_all(w_down, 'ep', split_axis=1, concat_axis=0, tiled=True)  34.1 us
    all_to_all x1, local copies, waits for them, and re-layouts, body(): lax.all_to_all(w_gate, 'ep', split_axis=1, concat_axis=0, tiled=True)  34.1 us
  transfers between devices with their start and end apart: 8, of which 6 were waited for; matrix products, arithmetic and copies ran while one was open for 44% of the time, Pallas kernels for 0%

commit v1 on v0

v1 whole, which is shorter than its diff:
```python
import functools

import jax
import jax.numpy as jnp
from jax import lax
from jax.experimental import pallas as pl
from jax.experimental.pallas import tpu as pltpu
from jax.sharding import PartitionSpec as P

QUARTERS = 4
MESH = pl.DeviceIdType.MESH


def kernel(
    n, tok, gw, src, wg, wu, wd, mixed, og, ou, od,
    p1a, p1b, p1c, picks, xall, gall, wv, acc, r1, part, s2, r2,
    p1_send, p1_recv, loc, p2_send, p2_recv, x_send, x_recv,
    tz_send, tz_recv, gz_send, gz_recv, tp_send, tp_recv, gp_send, gp_recv,
    a_send, a_recv, b_send, b_recv,
):
    planes = n // QUARTERS
    rows, width = tok.shape
    slots = og.shape[0]
    quarter = og.shape[1]
    piece = width // (2 * planes)
    me = lax.axis_index("ep")
    g = lax.axis_index("groups")
    z, c = me // QUARTERS, me % QUARTERS
    half = g % 2
    partner = g + 1 - 2 * half
    weights = (wg, wu, wd)
    outs = (og, ou, od)
    p1 = (p1a, p1b, p1c)

    barrier = pltpu.get_barrier_semaphore()

    def greet(k, _):
        pl.semaphore_signal(barrier, inc=1, device_id={"ep": (me + k) % n}, device_id_type=MESH)
        return 0

    lax.fori_loop(1, n, greet, 0)
    pl.semaphore_signal(barrier, inc=1, device_id={"groups": partner}, device_id_type=MESH)

    loads = [pltpu.make_async_copy(weights[m], wv.at[m], loc.at[m]) for m in range(3)]
    for load in loads:
        load.start()
    pl.semaphore_wait(barrier, n)

    def lanes(part_half, plane):
        return pl.ds(pl.multiple_of((part_half * planes + plane) * piece, 128), piece)

    def remote(a, b, send, recv, device):
        return pltpu.make_async_remote_copy(
            src_ref=a, dst_ref=b, send_sem=send, recv_sem=recv, device_id=device, device_id_type=MESH
        )

    def token_z(k, whose):
        other = (z + k) % planes
        device = {"ep": other * QUARTERS + c}
        return (
            remote(tok, xall.at[c, whose], tz_send.at[k], tz_recv.at[whose], device),
            remote(gw, gall.at[c, whose], gz_send.at[k], gz_recv.at[whose], device),
        )

    for k in range(1, planes):
        for copy in token_z(k, z):
            copy.start()
    xall[c, z] = tok[...]
    gall[c, z] = gw[...]

    def spread(m, k, whose):
        d = (me + k) % n
        dz, dc = d // QUARTERS, d % QUARTERS
        return remote(
            weights[m].at[pl.ds(pl.multiple_of(dc * quarter, 16), quarter), lanes(half, dz)],
            p1[m].at[whose], p1_send.at[m, k], p1_recv.at[m, whose], {"ep": d},
        )

    def keep(m):
        return pltpu.make_async_copy(
            weights[m].at[pl.ds(pl.multiple_of(c * quarter, 16), quarter), lanes(half, z)],
            p1[m].at[me], loc.at[3 + m],
        )

    for m in range(3):
        keep(m).start()

        def go(k, _):
            spread(m, k, me).start()
            return 0

        lax.fori_loop(1, n, go, 0)

    for k in range(1, planes):
        for copy in token_z(k, (z + k) % planes):
            copy.wait_recv()

    def token_p(k, whose):
        device = {"ep": z * QUARTERS + (c + k) % QUARTERS}
        return (
            remote(xall.at[whose], xall.at[whose], tp_send.at[k], tp_recv.at[whose], device),
            remote(gall.at[whose], gall.at[whose], gp_send.at[k], gp_recv.at[whose], device),
        )

    for k in range(1, QUARTERS):
        for copy in token_p(k, c):
            copy.start()

    def deliver(m, k, whose):
        q = (z + k) % planes
        return remote(
            picks.at[m, q], outs[m].at[:, :, lanes(half, whose)],
            p2_send.at[m, k], p2_recv.at[m, whose], {"ep": q * QUARTERS + c},
        )

    def settle(m):
        return pltpu.make_async_copy(picks.at[m, z], outs[m].at[:, :, lanes(half, z)], loc.at[6 + m])

    def across(m, part_half, whose, own):
        there = outs[m].at[:, :, lanes(part_half, whose)]
        return remote(
            picks.at[m, z] if own else there, there,
            x_send.at[m, whose], x_recv.at[m, whose], {"groups": partner},
        )

    def second(m):
        keep(m).wait()

        def arrive(k, _):
            spread(m, k, (me + k) % n).wait_recv()
            return 0

        lax.fori_loop(1, n, arrive, 0)

        def pick(i, _):
            picks[m, i // slots, i % slots] = p1[m][src[i]]
            return 0

        lax.fori_loop(0, planes * slots, pick, 0)
        for k in range(1, planes):
            deliver(m, k, z).start()
        settle(m).start()
        across(m, half, z, True).start()

    def forward(m):
        for k in range(1, planes):
            whose = (z + k) % planes
            deliver(m, k, whose).wait_recv()
            across(m, half, whose, False).start()

    total = planes * rows
    step = 256

    def expert(owner):
        x_lane = lax.broadcasted_iota(jnp.int32, (planes, rows, gall.shape[3]), 2)
        row_gate = jnp.sum(jnp.where(x_lane == me, gall[owner], 0.0), axis=2, keepdims=True)

        def unit(f, _):
            picked = xall[owner].reshape(total, width)
            cut = pl.ds(pl.multiple_of(f * step, step), step)
            dims = (((1,), (1,)), ((), ()))
            gate = lax.dot_general(picked, wv[0, cut, :], dims, preferred_element_type=jnp.float32)
            up = lax.dot_general(picked, wv[1, cut, :], dims, preferred_element_type=jnp.float32)
            hidden = (gate / (1.0 + jnp.exp(-gate)) * up).astype(jnp.bfloat16)
            made = jnp.dot(hidden, wv[2, cut, :], preferred_element_type=jnp.float32)
            acc[...] += made
            return 0

        acc[...] = jnp.zeros_like(acc)
        lax.fori_loop(0, wv.shape[1] // step, unit, 0)
        return (acc[...].reshape(planes, rows, width) * row_gate).astype(jnp.bfloat16)

    def add_plane(k, whose):
        return remote(
            part.at[k], r1.at[whose], a_send.at[k], a_recv.at[whose],
            {"ep": z * QUARTERS + (c + k) % QUARTERS},
        )

    def add_z(k, whose):
        other = (z + k) % planes
        return remote(
            s2.at[other], r2.at[whose], b_send.at[k], b_recv.at[whose],
            {"ep": other * QUARTERS + c},
        )

    second(0)
    second(1)

    for load in loads:
        load.wait()

    for k in range(1, QUARTERS):
        for copy in token_p(k, (c + k) % QUARTERS):
            copy.wait_recv()

    def work(k, _):
        part[k] = expert((c + k) % QUARTERS)

        @pl.when(k > 0)
        def _():
            add_plane(k, c).start()

        return 0

    lax.fori_loop(0, QUARTERS, work, 0)

    second(2)
    forward(0)

    for k in range(1, QUARTERS):
        add_plane(k, (c + k) % QUARTERS).wait_recv()

    def reduce_plane(i, _):
        summed = part[0, i].astype(jnp.float32)
        for k in range(1, QUARTERS):
            summed = summed + r1[(c + k) % QUARTERS, i].astype(jnp.float32)
        s2[i] = summed.astype(jnp.bfloat16)
        return 0

    lax.fori_loop(0, planes, reduce_plane, 0)
    for k in range(1, planes):
        add_z(k, z).start()

    forward(1)
    forward(2)

    result = s2[z].astype(jnp.float32)
    for k in range(1, planes):
        whose = (z + k) % planes
        add_z(k, whose).wait_recv()
        result = result + r2[whose].astype(jnp.float32)
    mixed[...] = result.astype(jnp.bfloat16)

    for k in range(1, planes):
        for copy in token_z(k, z):
            copy.wait_send()
        add_z(k, z).wait_send()
    for k in range(1, QUARTERS):
        for copy in token_p(k, c):
            copy.wait_send()
        add_plane(k, c).wait_send()
    for m in range(3):

        def sent(k, _):
            spread(m, k, me).wait_send()
            return 0

        lax.fori_loop(1, n, sent, 0)
        settle(m).wait()
        for k in range(1, planes):
            deliver(m, k, z).wait_send()
        across(m, half, z, True).wait_send()
        for k in range(1, planes):
            across(m, half, (z + k) % planes, False).wait_send()
        for k in range(planes):
            across(m, 1 - half, (z + k) % planes, False).wait_recv()


def body(tokens, routes, gate_codes, trainer_experts, placement, w_gate, w_up, w_down):
    n = lax.axis_size("ep")
    planes = n // QUARTERS
    rows, width = tokens.shape
    hidden_width = w_gate.shape[2]
    quarter = hidden_width // QUARTERS
    slots = placement.shape[1]
    piece = width // (2 * planes)
    codes = gate_codes.astype(jnp.float32)
    gate_values = codes / jnp.sum(codes, axis=1, keepdims=True)
    hits = routes[:, :, None] == trainer_experts[None, None, :]
    by_slot = jnp.sum(jnp.where(hits, gate_values[:, :, None], 0.0), axis=1)
    by_slot = jnp.pad(by_slot, ((0, 0), (0, 128 - n)))
    same = placement.reshape(-1)[:, None] == trainer_experts[None, :]
    source = jnp.sum(jnp.where(same, jnp.arange(n, dtype=jnp.int32)[None, :], 0), axis=1)
    flipped = [jnp.swapaxes(w[0], 0, 1) for w in (w_gate, w_up, w_down)]
    bf16 = jnp.bfloat16
    vmem = pl.BlockSpec(memory_space=pltpu.VMEM)
    hbm = pl.BlockSpec(memory_space=pl.ANY)
    slot_shape = jax.ShapeDtypeStruct((slots, quarter, width), bf16)
    dma = pltpu.SemaphoreType.DMA
    mixed, *moved = pl.pallas_call(
        functools.partial(kernel, n),
        out_shape=(jax.ShapeDtypeStruct((rows, width), bf16), slot_shape, slot_shape, slot_shape),
        in_specs=[vmem, vmem, pl.BlockSpec(memory_space=pltpu.SMEM), hbm, hbm, hbm],
        out_specs=(vmem, hbm, hbm, hbm),
        scratch_shapes=[
            pltpu.VMEM((n, quarter, piece), bf16),
            pltpu.VMEM((n, quarter, piece), bf16),
            pltpu.VMEM((n, quarter, piece), bf16),
            pltpu.VMEM((3, planes, slots, quarter, piece), bf16),
            pltpu.VMEM((QUARTERS, planes, rows, width), bf16),
            pltpu.VMEM((QUARTERS, planes, rows, 128), jnp.float32),
            pltpu.VMEM((3, hidden_width, width), bf16),
            pltpu.VMEM((planes * rows, width), jnp.float32),
            pltpu.VMEM((QUARTERS, planes, rows, width), bf16),
            pltpu.VMEM((QUARTERS, planes, rows, width), bf16),
            pltpu.VMEM((planes, rows, width), bf16),
            pltpu.VMEM((planes, rows, width), bf16),
            dma((3, n)), dma((3, n)), dma((9,)),
            dma((3, planes)), dma((3, planes)), dma((3, planes)), dma((3, planes)),
            dma((planes,)), dma((planes,)), dma((planes,)), dma((planes,)),
            dma((QUARTERS,)), dma((QUARTERS,)), dma((QUARTERS,)), dma((QUARTERS,)),
            dma((QUARTERS,)), dma((QUARTERS,)), dma((planes,)), dma((planes,)),
        ],
        compiler_params=pltpu.CompilerParams(
            collective_id=0, has_side_effects=True, vmem_limit_bytes=60 * 1024 * 1024
        ),
        cost_estimate=pl.CostEstimate(
            flops=6 * n * rows * width * hidden_width, bytes_accessed=40_000_000, transcendentals=0
        ),
    )(tokens, by_slot, source, *flipped)
    return (mixed, *(jnp.swapaxes(out, 1, 2)[None] for out in moved))


def solution(mesh):
    placed = (
        P(("groups", "ep"), None),
        P(("groups", "ep"), None),
        P(("groups", "ep"), None),
        P(),
        P(),
        P("ep", None, None),
        P("ep", None, None),
        P("ep", None, None),
    )
    return jax.shard_map(
        body,
        mesh=mesh,
        in_specs=placed,
        out_specs=(
            P(("groups", "ep"), None),
            P(("groups", "ep"), None, None, None),
            P(("groups", "ep"), None, None, None),
            P(("groups", "ep"), None, None, None),
        ),
        check_vma=False,
    )
```

time: 914 us -> 348 us (0.38); the launches traced: 904 us -> 348 us
  Pallas kernels: 0 us -> 318 us
  local copies, waits for them, and re-layouts: 313 us -> 25.6 us
  waiting for transfers between devices: 220 us -> 0 us
  other arithmetic: 178 us -> 3.53 us
  blocking collectives: 114 us -> 0 us
  starting transfers between devices: 40.4 us -> 0 us
  matrix products: 24.2 us -> 0 us
  between operations: 14.7 us -> 0.66 us
    pallas_call x0 -> x1, Pallas kernels: none -> 318 us  [body(): pl.pallas_call(functools.partial(kernel, n), out_shape=(jax.ShapeDtypeStr...]
    all_to_all x9 -> x0, local copies, waits for them, and re-layouts: 137 us -> none  [the longest x1 34.1 us: body(): lax.all_to_all(w_down, 'ep', split_axis=1, concat_axis=0, tiled=True)]
    unnamed x10 -> x0, other arithmetic: 134 us -> none
    all_to_all x6 -> x0, waiting for transfers between devices: 129 us -> none  [the longest x1 50 us: body(): lax.all_to_all(pick(moved_up), 'ep', split_axis=0, concat_axis=2, tiled=T...]
    all_gather x2 -> x0, blocking collectives: 114 us -> none  [the longest x1 97 us: body(): lax.all_gather(routes, 'ep', axis=0, tiled=True)]
    reduce_scatter x1 -> x0, waiting for transfers between devices: 90.4 us -> none  [body(): lax.psum_scatter(totals, 'ep', scatter_dimension=0, tiled=True)]
    gather x11 -> x0, local copies, waits for them, and re-layouts: 51.2 us -> none  [the longest x1 22.9 us: contribute(): picked = all_tokens[rows_index]]
    unnamed x33 -> x13, local copies, waits for them, and re-layouts: 69.9 us -> 24 us
  transfers between devices with their start and end apart: 8 -> 0, of which waited for: 6 -> 0; matrix products, arithmetic and copies ran while one was open for 44% -> 0% of each run, Pallas kernels for 0% -> 0%
where the time goes in v1:
time: 348 us
  Pallas kernels  318 us (91%)
  local copies, waits for them, and re-layouts  25.6 us (7%)
  other arithmetic  3.53 us (1%)
    pallas_call x1, Pallas kernels, body(): pl.pallas_call(functools.partial(kernel, n), out_shape=(jax.ShapeDtypeStr...  318 us
    unnamed x13, local copies, waits for them, and re-layouts  24 us

profile of v1, /device:TPU:8, one launch (start us, length us, event | category | flops | bytes accessed | tf_op | source)
XLA Modules:
  0.0 347.9 jit_solution(11151070376738820899)
XLA Ops:
  0.6 0.0 copy-start.2
  0.6 0.9 eq.31
  1.6 1.4 select_reduce_fusion.1.src
  2.9 0.7 convert_reduce_fusion
  3.6 0.7 convert_divide_fusion
  4.3 0.8 select_reduce_fusion
  5.1 0.1 copy.17
  5.2 0.6 pad.4.gw
  5.8 4.6 %copy.18 = bf16[1,2048,768]{1,2,0:T(8,128)(2,1)} copy(bf16[1,2048,768]{2,1,0:T(8,128)(2,1)} %param.13) | data formatting | bytes 6291456 | tf_op args[5]
  10.4 0.0 copy-done.2
  10.4 2.9 copy.19
  13.3 4.6 %copy.20 = bf16[1,2048,768]{1,2,0:T(8,128)(2,1)} copy(bf16[1,2048,768]{2,1,0:T(8,128)(2,1)} %param.15) | data formatting | bytes 6291456 | tf_op args[7]
  17.9 318.1 %shard_map.111 = (bf16[64,2048]{1,0:T(8,128)(2,1)}, bf16[5,192,2048]{2,1,0:T(8,128)(2,1)}, bf16[5,192,2048]{2,1,0:T(8,128)(2,1)}, bf16[5,192,2048]{2,1,0:T(8,128)(2,1)}) custom-call(bf16[64,2048]{1,0:T(8,128)(2,1)} %tok.1, f32[64,128]{1,0:T(8,128)} %pad.4.gw, s32[20]{0:T(128)} %select_reduce_fusion.1.src, bf16[768,2048]{1,0:T(8,128)(2,1)} %bitcast.21, ...), custom_call_target="tpu_custom_call" | custom-call | flops 9663676416 | bytes 40000000 | tf_op jit(solution)/shard_map/pallas_call | solution.py:280
  336.0 1.7 copy.25
  337.7 0.0 copy-start.1
  337.7 4.7 %copy.26 = bf16[1,5,2048,192]{2,3,1,0:T(8,128)(2,1)} copy(bf16[1,5,2048,192]{2,3,1,0:T(8,128)(2,1)} %bitcast.20) | data formatting | bytes 7864320
  342.4 0.0 copy-done.1
  342.4 0.0 copy-start
  342.4 2.0 copy.27
  344.4 1.5 copy-done
  346.0 1.9 copy.28
Async XLA Ops:
  0.6 9.8 %copy-start.2 = (bf16[1,2048,768]{2,1,0:T(8,128)(2,1)S(1)}, bf16[1,2048,768]{2,1,0:T(8,128)(2,1)}, u32[]{:S(2)}) copy-start(bf16[1,2048,768]{2,1,0:T(8,128)(2,1)} %param.14) | copy-start | bytes 9437188
  337.7 4.7 %copy-start.1 = (bf16[5,192,2048]{2,1,0:T(8,128)(2,1)S(1)}, bf16[5,192,2048]{2,1,0:T(8,128)(2,1)}, u32[]{:S(2)}) copy-start(bf16[5,192,2048]{2,1,0:T(8,128)(2,1)} %get-tuple-element.10) | copy-start | bytes 11796484
  342.4 3.5 %copy-start = (bf16[5,192,2048]{2,1,0:T(8,128)(2,1)S(1)}, bf16[5,192,2048]{2,1,0:T(8,128)(2,1)}, u32[]{:S(2)}) copy-start(bf16[5,192,2048]{2,1,0:T(8,128)(2,1)} %get-tuple-element.11) | copy-start | bytes 11796484

commit v2 on v1

--- a/solution.py
+++ b/solution.py
@@ -13,7 +13,7 @@
 
 def kernel(
     n, tok, gw, src, wg, wu, wd, mixed, og, ou, od,
-    p1a, p1b, p1c, picks, xall, gall, wv, acc, r1, part, s2, r2,
+    p1a, p1b, p1c, p1d, p1e, p1f, stage, picks, xall, gall, wv, acc, r1, part, s2, r2,
     p1_send, p1_recv, loc, p2_send, p2_recv, x_send, x_recv,
     tz_send, tz_recv, gz_send, gz_recv, tp_send, tp_recv, gp_send, gp_recv,
     a_send, a_recv, b_send, b_recv,
@@ -30,7 +30,9 @@
     partner = g + 1 - 2 * half
     weights = (wg, wu, wd)
     outs = (og, ou, od)
-    p1 = (p1a, p1b, p1c)
+    p1 = (p1a, p1b, p1c, p1d, p1e, p1f)
+    chunks = 6
+    band = quarter // 2
 
     barrier = pltpu.get_barrier_semaphore()
 
@@ -41,9 +43,10 @@
     lax.fori_loop(1, n, greet, 0)
     pl.semaphore_signal(barrier, inc=1, device_id={"groups": partner}, device_id_type=MESH)
 
-    loads = [pltpu.make_async_copy(weights[m], wv.at[m], loc.at[m]) for m in range(3)]
-    for load in loads:
-        load.start()
+    def load(m):
+        return pltpu.make_async_copy(weights[m], stage, loc.at[m])
+
+    load(0).start()
     pl.semaphore_wait(barrier, n)
 
     def lanes(part_half, plane):
@@ -68,28 +71,45 @@
     xall[c, z] = tok[...]
     gall[c, z] = gw[...]
 
-    def spread(m, k, whose):
+    def cut(t, dc, dz):
+        start = pl.multiple_of(dc * quarter + (t % 2) * band, 16)
+        return wv.at[t // 2, pl.ds(start, band), lanes(half, dz)]
+
+    def spread(t, k, whose):
         d = (me + k) % n
-        dz, dc = d // QUARTERS, d % QUARTERS
-        return remote(
-            weights[m].at[pl.ds(pl.multiple_of(dc * quarter, 16), quarter), lanes(half, dz)],
-            p1[m].at[whose], p1_send.at[m, k], p1_recv.at[m, whose], {"ep": d},
-        )
-
-    def keep(m):
-        return pltpu.make_async_copy(
-            weights[m].at[pl.ds(pl.multiple_of(c * quarter, 16), quarter), lanes(half, z)],
-            p1[m].at[me], loc.at[3 + m],
-        )
-
-    for m in range(3):
-        keep(m).start()
+        return remote(
+            cut(t, d % QUARTERS, d // QUARTERS),
+            p1[t].at[whose], p1_send.at[t, k], p1_recv.at[t, whose], {"ep": d},
+        )
+
+    def keep(t):
+        return pltpu.make_async_copy(cut(t, c, z), p1[t].at[me], loc.at[3 + t])
+
+    def flip(m):
+        load(m).wait()
+
+        def turn(i, _):
+            span = pl.ds(pl.multiple_of(i * 256, 256), 256)
+            wv[m, :, span] = jnp.swapaxes(stage[span, :], 0, 1)
+            return 0
+
+        lax.fori_loop(0, width // 256, turn, 0)
+        if m < 2:
+            load(m + 1).start()
+
+    def first(t):
+        keep(t).start()
 
         def go(k, _):
-            spread(m, k, me).start()
+            spread(t, k, me).start()
             return 0
 
         lax.fori_loop(1, n, go, 0)
+
+    flip(0)
+    first(0)
+    first(1)
+    flip(1)
 
     for k in range(1, planes):
         for copy in token_z(k, (z + k) % planes):
@@ -106,47 +126,50 @@
         for copy in token_p(k, c):
             copy.start()
 
-    def deliver(m, k, whose):
+    def target(t, part_half, whose):
+        return outs[t // 2].at[:, pl.ds((t % 2) * band, band), lanes(part_half, whose)]
+
+    def deliver(t, k, whose):
         q = (z + k) % planes
         return remote(
-            picks.at[m, q], outs[m].at[:, :, lanes(half, whose)],
-            p2_send.at[m, k], p2_recv.at[m, whose], {"ep": q * QUARTERS + c},
-        )
-
-    def settle(m):
-        return pltpu.make_async_copy(picks.at[m, z], outs[m].at[:, :, lanes(half, z)], loc.at[6 + m])
-
-    def across(m, part_half, whose, own):
-        there = outs[m].at[:, :, lanes(part_half, whose)]
-        return remote(
-            picks.at[m, z] if own else there, there,
-            x_send.at[m, whose], x_recv.at[m, whose], {"groups": partner},
-        )
-
-    def second(m):
-        keep(m).wait()
+            picks.at[t, q], target(t, half, whose),
+            p2_send.at[t, k], p2_recv.at[t, whose], {"ep": q * QUARTERS + c},
+        )
+
+    def settle(t):
+        return pltpu.make_async_copy(picks.at[t, z], target(t, half, z), loc.at[9 + t])
+
+    def across(t, part_half, whose, own):
+        there = target(t, part_half, whose)
+        return remote(
+            picks.at[t, z] if own else there, there,
+            x_send.at[t, whose], x_recv.at[t, whose], {"groups": partner},
+        )
+
+    def second(t):
+        keep(t).wait()
 
         def arrive(k, _):
-            spread(m, k, (me + k) % n).wait_recv()
+            spread(t, k, (me + k) % n).wait_recv()
             return 0
 
         lax.fori_loop(1, n, arrive, 0)
 
         def pick(i, _):
-            picks[m, i // slots, i % slots] = p1[m][src[i]]
+            picks[t, i // slots, i % slots] = p1[t][src[i]]
             return 0
 
         lax.fori_loop(0, planes * slots, pick, 0)
         for k in range(1, planes):
-            deliver(m, k, z).start()
-        settle(m).start()
-        across(m, half, z, True).start()
-
-    def forward(m):
+            deliver(t, k, z).start()
+        settle(t).start()
+        across(t, half, z, True).start()
+
+    def forward(t):
         for k in range(1, planes):
             whose = (z + k) % planes
-            deliver(m, k, whose).wait_recv()
-            across(m, half, whose, False).start()
+            deliver(t, k, whose).wait_recv()
+            across(t, half, whose, False).start()
 
     total = planes * rows
     step = 256
@@ -157,12 +180,12 @@
 
         def unit(f, _):
             picked = xall[owner].reshape(total, width)
-            cut = pl.ds(pl.multiple_of(f * step, step), step)
+            span = pl.ds(pl.multiple_of(f * step, step), step)
             dims = (((1,), (1,)), ((), ()))
-            gate = lax.dot_general(picked, wv[0, cut, :], dims, preferred_element_type=jnp.float32)
-            up = lax.dot_general(picked, wv[1, cut, :], dims, preferred_element_type=jnp.float32)
+            gate = lax.dot_general(picked, wv[0, span, :], dims, preferred_element_type=jnp.float32)
+            up = lax.dot_general(picked, wv[1, span, :], dims, preferred_element_type=jnp.float32)
             hidden = (gate / (1.0 + jnp.exp(-gate)) * up).astype(jnp.bfloat16)
-            made = jnp.dot(hidden, wv[2, cut, :], preferred_element_type=jnp.float32)
+            made = jnp.dot(hidden, wv[2, span, :], preferred_element_type=jnp.float32)
             acc[...] += made
             return 0
 
@@ -183,16 +206,6 @@
             {"ep": other * QUARTERS + c},
         )
 
-    second(0)
-    second(1)
-
-    for load in loads:
-        load.wait()
-
-    for k in range(1, QUARTERS):
-        for copy in token_p(k, (c + k) % QUARTERS):
-            copy.wait_recv()
-
     def work(k, _):
         part[k] = expert((c + k) % QUARTERS)
 
@@ -201,14 +214,6 @@
             add_plane(k, c).start()
 
         return 0
-
-    lax.fori_loop(0, QUARTERS, work, 0)
-
-    second(2)
-    forward(0)
-
-    for k in range(1, QUARTERS):
-        add_plane(k, (c + k) % QUARTERS).wait_recv()
 
     def reduce_plane(i, _):
         summed = part[0, i].astype(jnp.float32)
@@ -217,12 +222,32 @@
         s2[i] = summed.astype(jnp.bfloat16)
         return 0
 
+    first(2)
+    flip(2)
+    second(0)
+    first(3)
+    second(1)
+    first(4)
+    for k in range(1, QUARTERS):
+        for copy in token_p(k, (c + k) % QUARTERS):
+            copy.wait_recv()
+    lax.fori_loop(0, 2, work, 0)
+    second(2)
+    first(5)
+    forward(0)
+    lax.fori_loop(2, QUARTERS, work, 0)
+    second(3)
+    forward(1)
+    second(4)
+    for k in range(1, QUARTERS):
+        add_plane(k, (c + k) % QUARTERS).wait_recv()
     lax.fori_loop(0, planes, reduce_plane, 0)
     for k in range(1, planes):
         add_z(k, z).start()
-
-    forward(1)
     forward(2)
+    second(5)
+    for t in range(3, chunks):
+        forward(t)
 
     result = s2[z].astype(jnp.float32)
     for k in range(1, planes):
@@ -239,7 +264,7 @@
         for copy in token_p(k, c):
             copy.wait_send()
         add_plane(k, c).wait_send()
-    for m in range(3):
+    for m in range(chunks):
 
         def sent(k, _):
             spread(m, k, me).wait_send()
@@ -271,7 +296,6 @@
     by_slot = jnp.pad(by_slot, ((0, 0), (0, 128 - n)))
     same = placement.reshape(-1)[:, None] == trainer_experts[None, :]
     source = jnp.sum(jnp.where(same, jnp.arange(n, dtype=jnp.int32)[None, :], 0), axis=1)
-    flipped = [jnp.swapaxes(w[0], 0, 1) for w in (w_gate, w_up, w_down)]
     bf16 = jnp.bfloat16
     vmem = pl.BlockSpec(memory_space=pltpu.VMEM)
     hbm = pl.BlockSpec(memory_space=pl.ANY)
@@ -283,10 +307,14 @@
         in_specs=[vmem, vmem, pl.BlockSpec(memory_space=pltpu.SMEM), hbm, hbm, hbm],
         out_specs=(vmem, hbm, hbm, hbm),
         scratch_shapes=[
-            pltpu.VMEM((n, quarter, piece), bf16),
-            pltpu.VMEM((n, quarter, piece), bf16),
-            pltpu.VMEM((n, quarter, piece), bf16),
-            pltpu.VMEM((3, planes, slots, quarter, piece), bf16),
+            pltpu.VMEM((n, quarter // 2, piece), bf16),
+            pltpu.VMEM((n, quarter // 2, piece), bf16),
+            pltpu.VMEM((n, quarter // 2, piece), bf16),
+            pltpu.VMEM((n, quarter // 2, piece), bf16),
+            pltpu.VMEM((n, quarter // 2, piece), bf16),
+            pltpu.VMEM((n, quarter // 2, piece), bf16),
+            pltpu.VMEM((width, hidden_width), bf16),
+            pltpu.VMEM((6, planes, slots, quarter // 2, piece), bf16),
             pltpu.VMEM((QUARTERS, planes, rows, width), bf16),
             pltpu.VMEM((QUARTERS, planes, rows, 128), jnp.float32),
             pltpu.VMEM((3, hidden_width, width), bf16),
@@ -295,8 +323,8 @@
             pltpu.VMEM((QUARTERS, planes, rows, width), bf16),
             pltpu.VMEM((planes, rows, width), bf16),
             pltpu.VMEM((planes, rows, width), bf16),
-            dma((3, n)), dma((3, n)), dma((9,)),
-            dma((3, planes)), dma((3, planes)), dma((3, planes)), dma((3, planes)),
+            dma((6, n)), dma((6, n)), dma((15,)),
+            dma((6, planes)), dma((6, planes)), dma((6, planes)), dma((6, planes)),
             dma((planes,)), dma((planes,)), dma((planes,)), dma((planes,)),
             dma((QUARTERS,)), dma((QUARTERS,)), dma((QUARTERS,)), dma((QUARTERS,)),
             dma((QUARTERS,)), dma((QUARTERS,)), dma((planes,)), dma((planes,)),
@@ -307,7 +335,7 @@
         cost_estimate=pl.CostEstimate(
             flops=6 * n * rows * width * hidden_width, bytes_accessed=40_000_000, transcendentals=0
         ),
-    )(tokens, by_slot, source, *flipped)
+    )(tokens, by_slot, source, w_gate[0], w_up[0], w_down[0])
     return (mixed, *(jnp.swapaxes(out, 1, 2)[None] for out in moved))
 
 

time: 348 us -> 322 us (0.925)
  Pallas kernels: 318 us -> 305 us
  local copies, waits for them, and re-layouts: 25.6 us -> 13.3 us
    pallas_call x1, Pallas kernels: 318 us -> 305 us  [body(): pl.pallas_call(functools.partial(kernel, n), out_shape=(jax.ShapeDtypeStr...]
    unnamed x13 -> x8, local copies, waits for them, and re-layouts: 24 us -> 11.9 us
where the time goes in v2:
time: 322 us
  Pallas kernels  305 us (95%)
  local copies, waits for them, and re-layouts  13.3 us (4%)
  other arithmetic  3.42 us (1%)
    pallas_call x1, Pallas kernels, body(): pl.pallas_call(functools.partial(kernel, n), out_shape=(jax.ShapeDtypeStr...  305 us
    unnamed x8, local copies, waits for them, and re-layouts  11.9 us

profile of v2, /device:TPU:8, one launch (start us, length us, event | category | flops | bytes accessed | tf_op | source)
XLA Modules:
  0.0 321.9 jit_solution(10430961866749684317)
XLA Ops:
  0.6 0.8 eq.31
  1.4 1.3 select_reduce_fusion.1.src
  2.6 0.7 convert_reduce_fusion
  3.4 0.7 convert_divide_fusion
  4.0 0.8 select_reduce_fusion
  4.8 0.1 copy.14
  4.9 0.6 pad.4.gw
  5.5 304.5 %shard_map.111 = (bf16[64,2048]{1,0:T(8,128)(2,1)}, bf16[5,192,2048]{2,1,0:T(8,128)(2,1)}, bf16[5,192,2048]{2,1,0:T(8,128)(2,1)}, bf16[5,192,2048]{2,1,0:T(8,128)(2,1)}) custom-call(bf16[64,2048]{1,0:T(8,128)(2,1)} %tok.1, f32[64,128]{1,0:T(8,128)} %pad.4.gw, s32[20]{0:T(128)} %select_reduce_fusion.1.src, bf16[2048,768]{1,0:T(8,128)(2,1)} %bitcast.15, ...), custom_call_target="tpu_custom_call" | custom-call | flops 9663676416 | bytes 40000000 | tf_op jit(solution)/shard_map/pallas_call | solution.py:304
  310.1 1.7 copy.19
  311.7 0.0 copy-start.1
  311.7 4.7 %copy.20 = bf16[1,5,2048,192]{2,3,1,0:T(8,128)(2,1)} copy(bf16[1,5,2048,192]{2,3,1,0:T(8,128)(2,1)} %bitcast.14) | data formatting | bytes 7864320
  316.5 0.0 copy-done.1
  316.5 0.0 copy-start
  316.5 2.0 copy.21
  318.5 1.5 copy-done
  320.0 1.9 copy.22
Async XLA Ops:
  311.7 4.7 %copy-start.1 = (bf16[5,192,2048]{2,1,0:T(8,128)(2,1)S(1)}, bf16[5,192,2048]{2,1,0:T(8,128)(2,1)}, u32[]{:S(2)}) copy-start(bf16[5,192,2048]{2,1,0:T(8,128)(2,1)} %get-tuple-element.10) | copy-start | bytes 11796484
  316.5 3.5 %copy-start = (bf16[5,192,2048]{2,1,0:T(8,128)(2,1)S(1)}, bf16[5,192,2048]{2,1,0:T(8,128)(2,1)}, u32[]{:S(2)}) copy-start(bf16[5,192,2048]{2,1,0:T(8,128)(2,1)} %get-tuple-element.11) | copy-start | bytes 11796484

commit v3 on v2

--- a/solution.py
+++ b/solution.py
@@ -57,19 +57,40 @@
             src_ref=a, dst_ref=b, send_sem=send, recv_sem=recv, device_id=device, device_id_type=MESH
         )
 
-    def token_z(k, whose):
-        other = (z + k) % planes
-        device = {"ep": other * QUARTERS + c}
+    def hop(plane, offset):
+        for bit in strides:
+            if offset & bit:
+                plane = plane + bit - 2 * bit * ((plane // bit) % 2)
+        return plane
+
+    strides = [1 << i for i in range(planes.bit_length() - 1)]
+    gathers, sums = [], []
+    for bit in reversed(strides):
+        gathers.append([(bit, o) for o in range(planes) if o % (2 * bit) == 0])
+    for bit in strides:
+        sums.append([(bit, o) for o in range(planes) if o % (2 * bit) == bit])
+
+    def token_z(bit, o, arriving):
+        whose = hop(z, bit ^ o) if arriving else hop(z, o)
+        device = {"ep": hop(z, bit) * QUARTERS + c}
         return (
-            remote(tok, xall.at[c, whose], tz_send.at[k], tz_recv.at[whose], device),
-            remote(gw, gall.at[c, whose], gz_send.at[k], gz_recv.at[whose], device),
-        )
-
-    for k in range(1, planes):
-        for copy in token_z(k, z):
-            copy.start()
+            remote(xall.at[c, whose], xall.at[c, whose], tz_send.at[bit ^ o], tz_recv.at[whose], device),
+            remote(gall.at[c, whose], gall.at[c, whose], gz_send.at[bit ^ o], gz_recv.at[whose], device),
+        )
+
+    def gather_start(stage_index):
+        for bit, o in gathers[stage_index]:
+            for copy in token_z(bit, o, False):
+                copy.start()
+
+    def gather_wait(stage_index):
+        for bit, o in gathers[stage_index]:
+            for copy in token_z(bit, o, True):
+                copy.wait_recv()
+
     xall[c, z] = tok[...]
     gall[c, z] = gw[...]
+    gather_start(0)
 
     def cut(t, dc, dz):
         start = pl.multiple_of(dc * quarter + (t % 2) * band, 16)
@@ -109,11 +130,11 @@
     flip(0)
     first(0)
     first(1)
+    for i in range(1, len(gathers)):
+        gather_wait(i - 1)
+        gather_start(i)
     flip(1)
-
-    for k in range(1, planes):
-        for copy in token_z(k, (z + k) % planes):
-            copy.wait_recv()
+    gather_wait(len(gathers) - 1)
 
     def token_p(k, whose):
         device = {"ep": z * QUARTERS + (c + k) % QUARTERS}
@@ -199,12 +220,21 @@
             {"ep": z * QUARTERS + (c + k) % QUARTERS},
         )
 
-    def add_z(k, whose):
-        other = (z + k) % planes
-        return remote(
-            s2.at[other], r2.at[whose], b_send.at[k], b_recv.at[whose],
-            {"ep": other * QUARTERS + c},
-        )
+    def add_z(bit, o):
+        return remote(
+            s2.at[hop(z, o)], r2.at[o], b_send.at[o], b_recv.at[o],
+            {"ep": hop(z, bit) * QUARTERS + c},
+        )
+
+    def sum_start(stage_index):
+        for bit, o in sums[stage_index]:
+            add_z(bit, o).start()
+
+    def sum_fold(stage_index):
+        for bit, o in sums[stage_index]:
+            add_z(bit, o).wait_recv()
+            home = hop(z, o ^ bit)
+            s2[home] = (s2[home].astype(jnp.float32) + r2[o].astype(jnp.float32)).astype(jnp.bfloat16)
 
     def work(k, _):
         part[k] = expert((c + k) % QUARTERS)
@@ -242,24 +272,27 @@
     for k in range(1, QUARTERS):
         add_plane(k, (c + k) % QUARTERS).wait_recv()
     lax.fori_loop(0, planes, reduce_plane, 0)
-    for k in range(1, planes):
-        add_z(k, z).start()
+    sum_start(0)
     forward(2)
     second(5)
+    for i in range(1, len(sums)):
+        sum_fold(i - 1)
+        sum_start(i)
     for t in range(3, chunks):
         forward(t)
 
-    result = s2[z].astype(jnp.float32)
-    for k in range(1, planes):
-        whose = (z + k) % planes
-        add_z(k, whose).wait_recv()
-        result = result + r2[whose].astype(jnp.float32)
+    bit, last = sums[-1][0]
+    add_z(bit, last).wait_recv()
+    result = s2[z].astype(jnp.float32) + r2[last].astype(jnp.float32)
     mixed[...] = result.astype(jnp.bfloat16)
 
-    for k in range(1, planes):
-        for copy in token_z(k, z):
-            copy.wait_send()
-        add_z(k, z).wait_send()
+    for stage_list in gathers:
+        for bit, o in stage_list:
+            for copy in token_z(bit, o, False):
+                copy.wait_send()
+    for stage_list in sums:
+        for bit, o in stage_list:
+            add_z(bit, o).wait_send()
     for k in range(1, QUARTERS):
         for copy in token_p(k, c):
             copy.wait_send()

time: 322 us -> 305 us (0.947)
  Pallas kernels: 305 us -> 287 us
    pallas_call x1, Pallas kernels: 305 us -> 287 us  [body(): pl.pallas_call(functools.partial(kernel, n), out_shape=(jax.ShapeDtypeStr...]
where the time goes in v3:
time: 305 us
  Pallas kernels  287 us (94%)
  local copies, waits for them, and re-layouts  13.3 us (4%)
  other arithmetic  3.42 us (1%)
    pallas_call x1, Pallas kernels, body(): pl.pallas_call(functools.partial(kernel, n), out_shape=(jax.ShapeDtypeStr...  287 us
    unnamed x8, local copies, waits for them, and re-layouts  11.9 us

profile of v3, /device:TPU:8, one launch (start us, length us, event | category | flops | bytes accessed | tf_op | source)
XLA Modules:
  0.0 304.6 jit_solution(11709310849956792245)
XLA Ops:
  0.6 0.8 eq.31
  1.4 1.3 select_reduce_fusion.1.src
  2.6 0.7 convert_reduce_fusion
  3.4 0.7 convert_divide_fusion
  4.0 0.8 select_reduce_fusion
  4.8 0.1 copy.14
  4.9 0.6 pad.4.gw
  5.5 287.2 %shard_map.111 = (bf16[64,2048]{1,0:T(8,128)(2,1)}, bf16[5,192,2048]{2,1,0:T(8,128)(2,1)}, bf16[5,192,2048]{2,1,0:T(8,128)(2,1)}, bf16[5,192,2048]{2,1,0:T(8,128)(2,1)}) custom-call(bf16[64,2048]{1,0:T(8,128)(2,1)} %tok.1, f32[64,128]{1,0:T(8,128)} %pad.4.gw, s32[20]{0:T(128)} %select_reduce_fusion.1.src, bf16[2048,768]{1,0:T(8,128)(2,1)} %bitcast.15, ...), custom_call_target="tpu_custom_call" | custom-call | flops 9663676416 | bytes 40000000 | tf_op jit(solution)/shard_map/pallas_call | solution.py:337
  292.8 1.7 copy.19
  294.4 0.0 copy-start.1
  294.4 4.7 %copy.20 = bf16[1,5,2048,192]{2,3,1,0:T(8,128)(2,1)} copy(bf16[1,5,2048,192]{2,3,1,0:T(8,128)(2,1)} %bitcast.14) | data formatting | bytes 7864320
  299.2 0.0 copy-done.1
  299.2 0.0 copy-start
  299.2 2.0 copy.21
  301.2 1.5 copy-done
  302.7 1.9 copy.22
Async XLA Ops:
  294.4 4.7 %copy-start.1 = (bf16[5,192,2048]{2,1,0:T(8,128)(2,1)S(1)}, bf16[5,192,2048]{2,1,0:T(8,128)(2,1)}, u32[]{:S(2)}) copy-start(bf16[5,192,2048]{2,1,0:T(8,128)(2,1)} %get-tuple-element.10) | copy-start | bytes 11796484
  299.2 3.5 %copy-start = (bf16[5,192,2048]{2,1,0:T(8,128)(2,1)S(1)}, bf16[5,192,2048]{2,1,0:T(8,128)(2,1)}, u32[]{:S(2)}) copy-start(bf16[5,192,2048]{2,1,0:T(8,128)(2,1)} %get-tuple-element.11) | copy-start | bytes 11796484

commit v4 on v3

--- a/solution.py
+++ b/solution.py
@@ -188,7 +188,7 @@
 
     def forward(t):
         for k in range(1, planes):
-            whose = (z + k) % planes
+            whose = hop(z, k)
             deliver(t, k, whose).wait_recv()
             across(t, half, whose, False).start()
 
@@ -226,6 +226,9 @@
             {"ep": hop(z, bit) * QUARTERS + c},
         )
 
+    def strip(home):
+        return pl.ds(pl.multiple_of(home * rows, rows), rows)
+
     def sum_start(stage_index):
         for bit, o in sums[stage_index]:
             add_z(bit, o).start()
@@ -234,7 +237,9 @@
         for bit, o in sums[stage_index]:
             add_z(bit, o).wait_recv()
             home = hop(z, o ^ bit)
-            s2[home] = (s2[home].astype(jnp.float32) + r2[o].astype(jnp.float32)).astype(jnp.bfloat16)
+            summed = acc[strip(home), :] + r2[o].astype(jnp.float32)
+            acc[strip(home), :] = summed
+            s2[home] = summed.astype(jnp.bfloat16)
 
     def work(k, _):
         part[k] = expert((c + k) % QUARTERS)
@@ -249,6 +254,7 @@
         summed = part[0, i].astype(jnp.float32)
         for k in range(1, QUARTERS):
             summed = summed + r1[(c + k) % QUARTERS, i].astype(jnp.float32)
+        acc[strip(i), :] = summed
         s2[i] = summed.astype(jnp.bfloat16)
         return 0
 
@@ -283,7 +289,7 @@
 
     bit, last = sums[-1][0]
     add_z(bit, last).wait_recv()
-    result = s2[z].astype(jnp.float32) + r2[last].astype(jnp.float32)
+    result = acc[strip(z), :] + r2[last].astype(jnp.float32)
     mixed[...] = result.astype(jnp.bfloat16)
 
     for stage_list in gathers:

time: 305 us -> 296 us (0.970)
  Pallas kernels: 287 us -> 277 us
    pallas_call x1, Pallas kernels: 287 us -> 277 us  [body(): pl.pallas_call(functools.partial(kernel, n), out_shape=(jax.ShapeDtypeStr...]
where the time goes in v4:
time: 296 us; the launch traced here: 294 us
  Pallas kernels  277 us (94%)
  local copies, waits for them, and re-layouts  13.3 us (4%)
  other arithmetic  3.42 us (1%)
    pallas_call x1, Pallas kernels, body(): pl.pallas_call(functools.partial(kernel, n), out_shape=(jax.ShapeDtypeStr...  277 us
    unnamed x8, local copies, waits for them, and re-layouts  11.9 us

profile of v4, /device:TPU:8, one launch (start us, length us, event | category | flops | bytes accessed | tf_op | source)
XLA Modules:
  0.0 294.1 jit_solution(1567750564939688590)
XLA Ops:
  0.6 0.8 eq.31
  1.4 1.3 select_reduce_fusion.1.src
  2.6 0.7 convert_reduce_fusion
  3.4 0.7 convert_divide_fusion
  4.0 0.8 select_reduce_fusion
  4.8 0.1 copy.14
  4.9 0.6 pad.4.gw
  5.5 276.7 %shard_map.111 = (bf16[64,2048]{1,0:T(8,128)(2,1)}, bf16[5,192,2048]{2,1,0:T(8,128)(2,1)}, bf16[5,192,2048]{2,1,0:T(8,128)(2,1)}, bf16[5,192,2048]{2,1,0:T(8,128)(2,1)}) custom-call(bf16[64,2048]{1,0:T(8,128)(2,1)} %tok.1, f32[64,128]{1,0:T(8,128)} %pad.4.gw, s32[20]{0:T(128)} %select_reduce_fusion.1.src, bf16[2048,768]{1,0:T(8,128)(2,1)} %bitcast.15, ...), custom_call_target="tpu_custom_call" | custom-call | flops 9663676416 | bytes 40000000 | tf_op jit(solution)/shard_map/pallas_call | solution.py:343
  282.2 1.7 copy.19
  283.9 0.0 copy-start.1
  283.9 4.7 %copy.20 = bf16[1,5,2048,192]{2,3,1,0:T(8,128)(2,1)} copy(bf16[1,5,2048,192]{2,3,1,0:T(8,128)(2,1)} %bitcast.14) | data formatting | bytes 7864320
  288.6 0.0 copy-done.1
  288.6 0.0 copy-start
  288.6 2.0 copy.21
  290.6 1.5 copy-done
  292.2 1.9 copy.22
Async XLA Ops:
  283.9 4.7 %copy-start.1 = (bf16[5,192,2048]{2,1,0:T(8,128)(2,1)S(1)}, bf16[5,192,2048]{2,1,0:T(8,128)(2,1)}, u32[]{:S(2)}) copy-start(bf16[5,192,2048]{2,1,0:T(8,128)(2,1)} %get-tuple-element.10) | copy-start | bytes 11796484
  288.6 3.5 %copy-start = (bf16[5,192,2048]{2,1,0:T(8,128)(2,1)S(1)}, bf16[5,192,2048]{2,1,0:T(8,128)(2,1)}, u32[]{:S(2)}) copy-start(bf16[5,192,2048]{2,1,0:T(8,128)(2,1)} %get-tuple-element.11) | copy-start | bytes 11796484
